TPU v7x, 32 devices: a whole 2x2x4 slice. The times are simulated.
32 devices in a mesh: fsdp: 8 (over z, core), ctx: 2 (over x), tp: 2 (over y).
Axes of the slice: x: 2, y: 2, z: 4, core: 2. Of those that a mesh axis runs over, the one named last changes fastest.
Arguments:
- tokens: bfloat16 [9216, 768], P(('fsdp', 'ctx')), may hold values from -6 to 6
- norm1_gain: bfloat16 [768], P('fsdp'), may hold values from 0.5 to 1.5
- w_qkv: bfloat16 [768, 3, 768], P('fsdp', None, 'tp'), may hold values from -0.21875 to 0.21875
- w_out: bfloat16 [768, 768], P('tp', 'fsdp'), may hold values from -0.875 to 0.875
- rel_bias: bfloat16 [32, 12], P('fsdp', 'tp'), may hold values from -3 to 3
- norm2_gain: bfloat16 [768], P('fsdp'), may hold values from 0.5 to 1.5
- w_up: bfloat16 [8, 768, 3072], P('fsdp', 'ctx', 'tp'), may hold values from -0.21875 to 0.21875
- w_down: bfloat16 [8, 3072, 768], P('fsdp', 'tp', 'ctx'), may hold values from -0.109375 to 0.109375
- gates: float32 [9216, 2], P(('fsdp', 'ctx')), may hold values from 0.2 to 0.8
- routes: int32 [9216, 2], P(('fsdp', 'ctx')), may hold values from 0 to 7, all different within a row; in each aligned block of 576 rows (0 to 575, 576 to 1151, ...) at most 288 rows name the same one
- lengths: int32 [8, 3], P('fsdp'), may hold values from 1 to 1024, 1152 in all within a row
- buckets: int32 [1152], replicated, may hold values from 0 to 31
- grad_out: float32 [9216, 768], P(('fsdp', 'ctx')), may hold values from -6 to 6
Outputs:
- output: float32 [9216, 768], P(('fsdp', 'ctx'))
- grad_tokens: float32 [9216, 768], P(('fsdp', 'ctx'))
- grad_norm1_gain: float32 [768], P('fsdp')
- grad_w_qkv: float32 [768, 3, 768], P('fsdp', None, 'tp')
- grad_w_out: float32 [768, 768], P('tp', 'fsdp')
- grad_rel_bias: float32 [32, 12], P('fsdp', 'tp')
- grad_norm2_gain: float32 [768], P('fsdp')
- grad_w_up: float32 [8, 768, 3072], P('fsdp', 'ctx', 'tp')
- grad_w_down: float32 [8, 3072, 768], P('fsdp', 'tp', 'ctx')
Inputs may be any that keep to these rules, and one draw needn't show every extreme that they name: `routes`: each row names 2 different experts; in the rows of one device (aligned blocks of 576 rows) no expert is named more than 288 times. `lengths`: each row sums to 1152; its largest entry is 1024.
All inputs are finite; a program needn't handle non-finite values.
Results may differ from a plain program's by a relative error of at most 0.02.
Values may be sent and summed in bfloat16 or wider, within the bound.
A program may use at most 192 MiB of HBM per device.

v0:
```python
import jax
import jax.numpy as jnp
from jax import lax
from jax.sharding import PartitionSpec as P

HEAD_DIM = 64
TOP = 2


eps = 1e-06


def norm_forward(values, gain_vec):
    inverse = lax.rsqrt(jnp.mean(values * values, axis=-1, keepdims=True) + eps)
    normal = values * inverse
    return (normal * gain_vec, normal, inverse)


def norm_backward(upstream, gain_vec, normal, inverse):
    gain_grad = jnp.sum(upstream * normal, axis=0)
    scaled = upstream * gain_vec
    input_grad = inverse * (scaled - normal * jnp.mean(scaled * normal, axis=-1, keepdims=True))
    return (input_grad, gain_grad)


def to_experts(rows_flat, fsdp_size, exp_dev, capacity, width):
    return (
        rows_flat.reshape(fsdp_size, exp_dev, capacity, width)
        .transpose(1, 0, 2, 3)
        .reshape(exp_dev, fsdp_size * capacity, width)
    )


def from_experts(rows_exp, fsdp_size, exp_dev, capacity, width):
    return (
        rows_exp.reshape(exp_dev, fsdp_size, capacity, width)
        .transpose(1, 0, 2, 3)
        .reshape(fsdp_size, exp_dev * capacity, width)
    )


def pair_buckets(buckets, group_len, q_start, q_count, k_start, k_count):
    padded = jnp.concatenate((jnp.zeros((group_len,), jnp.int32), buckets))
    flipped = padded[::-1]
    span = q_count + k_count
    first = group_len - q_start + k_start - q_count
    window = lax.dynamic_slice_in_dim(flipped, first, span)
    rolled = jnp.concatenate((window[q_count - 1 :], window[: q_count - 1]))
    tiled = jnp.tile(rolled, q_count)[: q_count * (span - 1)].reshape(q_count, span - 1)
    return tiled[:, :k_count]


def pair_terms(query_pos, key_pos, seq_ends, buckets, bias_table, group_len, q_start, k_start):
    query_seq = jnp.sum((query_pos[:, None] >= seq_ends[None, :]).astype(jnp.int32), axis=1)
    key_seq = jnp.sum((key_pos[:, None] >= seq_ends[None, :]).astype(jnp.int32), axis=1)
    allowed = (query_seq[:, None] == key_seq[None, :]) & (key_pos[None, :] <= query_pos[:, None])
    bucket_ids = pair_buckets(
        buckets, group_len, q_start, query_pos.shape[0], k_start, key_pos.shape[0]
    )
    pair_hot = (
        bucket_ids[:, :, None] == jnp.arange(bias_table.shape[0], dtype=jnp.int32)[None, None, :]
    ).astype(jnp.bfloat16)
    bias_full = jnp.einsum("qkb,bh->hqk", pair_hot, bias_table, preferred_element_type=jnp.float32)
    return (allowed, pair_hot, bias_full)


def body(
    tokens,
    norm1_gain,
    w_qkv,
    w_out,
    rel_bias,
    norm2_gain,
    w_up,
    w_down,
    gates,
    routes,
    lengths,
    buckets,
    grad_out,
):
    tok_count = tokens.shape[0]
    width = tokens.shape[1]
    ctx_size = lax.axis_size("ctx")
    fsdp_size = lax.axis_size("fsdp")
    group_len = tok_count * ctx_size
    exp_dev = w_up.shape[0]
    score_scale = HEAD_DIM ** (-0.5)
    gain_one, qkv_weight, out_weight, bias_table, gain_two = (
        lax.all_gather(norm1_gain, "fsdp", axis=0, tiled=True),
        lax.all_gather(w_qkv, "fsdp", axis=0, tiled=True),
        lax.all_gather(w_out, "fsdp", axis=1, tiled=True),
        lax.all_gather(rel_bias, "fsdp", axis=0, tiled=True),
        lax.all_gather(norm2_gain, "fsdp", axis=0, tiled=True),
    )
    gain_one = gain_one.astype(jnp.float32)
    gain_two = gain_two.astype(jnp.float32)
    feat_local = qkv_weight.shape[2]
    local_heads = feat_local // HEAD_DIM
    inputs = tokens.astype(jnp.float32)
    normed_one, normal_one, inverse_one = norm_forward(inputs, gain_one)
    normed_low = normed_one.astype(jnp.bfloat16)
    project = jnp.einsum(
        "td,dcf->tcf", normed_low, qkv_weight, preferred_element_type=jnp.float32
    ).astype(jnp.bfloat16)
    queries = project[:, 0].reshape(tok_count, local_heads, HEAD_DIM)
    key_value = lax.all_gather(project[:, 1:], "ctx", axis=0, tiled=True)
    keys_all = key_value[:, 0].reshape(group_len, local_heads, HEAD_DIM)
    values_all = key_value[:, 1].reshape(group_len, local_heads, HEAD_DIM)
    block_start = lax.axis_index("ctx") * tok_count
    query_pos = block_start + jnp.arange(tok_count, dtype=jnp.int32)
    key_pos = jnp.arange(group_len, dtype=jnp.int32)
    seq_ends = jnp.cumsum(lengths[0])
    allowed, pair_hot, bias_full = pair_terms(
        query_pos, key_pos, seq_ends, buckets, bias_table, group_len, block_start, 0
    )
    scores = (
        jnp.einsum("qhd,khd->hqk", queries, keys_all, preferred_element_type=jnp.float32)
        * score_scale
        + bias_full
    )
    scores = jnp.where(allowed[None], scores, -1e30)
    highest = jnp.max(scores, axis=-1, keepdims=True)
    weights = jnp.exp(scores - highest)
    total = jnp.sum(weights, axis=-1, keepdims=True)
    attn_probs = weights / total
    probs_low = attn_probs.astype(jnp.bfloat16)
    attended = jnp.einsum("hqk,khd->qhd", probs_low, values_all, preferred_element_type=jnp.float32)
    attended_low = attended.astype(jnp.bfloat16).reshape(tok_count, feat_local)
    attn_branch = lax.psum(
        jnp.dot(attended_low, out_weight, preferred_element_type=jnp.float32).astype(jnp.bfloat16),
        "tp",
    ).astype(jnp.float32)
    middle = inputs + attn_branch
    normed_two, normal_two, inverse_two = norm_forward(middle, gain_two)
    normed_two_low = normed_two.astype(jnp.bfloat16)
    experts_total = exp_dev * fsdp_size
    capacity = 2 * tok_count * TOP // experts_total
    slot_count = experts_total * capacity
    choices_flat = routes.reshape(-1)
    expert_hot = (
        choices_flat[:, None] == jnp.arange(experts_total, dtype=jnp.int32)[None, :]
    ).astype(jnp.int32)
    slot_place = jnp.sum((jnp.cumsum(expert_hot, axis=0) - 1) * expert_hot, axis=1)
    slot_index = choices_flat * capacity + slot_place
    assign_hot = slot_index[None, :] == jnp.arange(slot_count, dtype=jnp.int32)[:, None]
    token_of = jnp.arange(tok_count * TOP, dtype=jnp.int32) // TOP
    slot_token = jnp.sum(jnp.where(assign_hot, token_of[None, :], 0), axis=1)
    gate_slot = jnp.sum(jnp.where(assign_hot, gates.reshape(-1)[None, :], 0.0), axis=1)
    dispatch = jnp.any(assign_hot.reshape(slot_count, tok_count, TOP), axis=2).astype(jnp.bfloat16)
    send_rows = jnp.dot(dispatch, normed_two_low, preferred_element_type=jnp.float32).astype(
        jnp.bfloat16
    )
    received = lax.all_to_all(
        send_rows.reshape(fsdp_size, exp_dev * capacity, width),
        "fsdp",
        split_axis=0,
        concat_axis=0,
        tiled=True,
    )
    expert_rows = to_experts(received, fsdp_size, exp_dev, capacity, width)
    up_full, down_full = (
        lax.all_gather(w_up, "ctx", axis=1, tiled=True),
        lax.all_gather(w_down, "ctx", axis=2, tiled=True),
    )
    inner_act = jnp.einsum("erd,edf->erf", expert_rows, up_full, preferred_element_type=jnp.float32)
    hidden_low = jax.nn.gelu(inner_act).astype(jnp.bfloat16)
    partial_out = jnp.einsum(
        "erf,efd->erd", hidden_low, down_full, preferred_element_type=jnp.float32
    )
    expert_out = lax.psum(partial_out.astype(jnp.bfloat16), "tp")
    returned = lax.all_to_all(
        from_experts(expert_out, fsdp_size, exp_dev, capacity, width),
        "fsdp",
        split_axis=0,
        concat_axis=0,
        tiled=True,
    ).reshape(slot_count, width)
    picked = returned[slot_index].astype(jnp.float32).reshape(tok_count, TOP, width)
    mixture = jnp.sum(gates[:, :, None] * picked, axis=1)
    output = middle + mixture
    slot_grad = (gate_slot[:, None] * grad_out[slot_token]).astype(jnp.bfloat16)
    grad_rows = lax.all_to_all(
        slot_grad.reshape(fsdp_size, exp_dev * capacity, width),
        "fsdp",
        split_axis=0,
        concat_axis=0,
        tiled=True,
    )
    grad_expert = to_experts(grad_rows, fsdp_size, exp_dev, capacity, width)
    grad_hidden = jnp.einsum(
        "erd,efd->erf", grad_expert, down_full, preferred_element_type=jnp.float32
    )
    gelu_value, gelu_pull = jax.vjp(jax.nn.gelu, inner_act)
    grad_inner = gelu_pull(grad_hidden)[0].astype(jnp.bfloat16)
    grad_down_local = jnp.einsum(
        "erf,erd->efd", hidden_low, grad_expert, preferred_element_type=jnp.float32
    )
    grad_up_local = jnp.einsum(
        "erd,erf->edf", expert_rows, grad_inner, preferred_element_type=jnp.float32
    )
    row_grad_part = jnp.einsum(
        "erf,edf->erd", grad_inner, up_full, preferred_element_type=jnp.float32
    )
    row_grad = lax.psum(row_grad_part.astype(jnp.bfloat16), "tp")
    returned_grad = lax.all_to_all(
        from_experts(row_grad, fsdp_size, exp_dev, capacity, width),
        "fsdp",
        split_axis=0,
        concat_axis=0,
        tiled=True,
    ).reshape(slot_count, width)
    grad_normed_two = jnp.dot(dispatch.T, returned_grad, preferred_element_type=jnp.float32)
    grad_from_two, gain_two_grad = norm_backward(grad_normed_two, gain_two, normal_two, inverse_two)
    grad_middle = grad_out + grad_from_two
    grad_branch = grad_middle.astype(jnp.bfloat16)
    grad_out_weight = jnp.dot(attended_low.T, grad_branch, preferred_element_type=jnp.float32)
    grad_attended = (
        jnp.dot(grad_branch, out_weight.T, preferred_element_type=jnp.float32)
        .astype(jnp.bfloat16)
        .reshape(tok_count, local_heads, HEAD_DIM)
    )
    grad_probs = jnp.einsum(
        "qhd,khd->hqk", grad_attended, values_all, preferred_element_type=jnp.float32
    )
    row_dot = jnp.sum(attn_probs * grad_probs, axis=-1)
    grad_scores = attn_probs * (grad_probs - row_dot[:, :, None])
    scores_low = grad_scores.astype(jnp.bfloat16)
    grad_queries = (
        jnp.einsum("hqk,khd->qhd", scores_low, keys_all, preferred_element_type=jnp.float32)
        * score_scale
    ).astype(jnp.bfloat16)
    bias_grad = jnp.einsum("hqk,qkb->bh", scores_low, pair_hot, preferred_element_type=jnp.float32)
    grad_values = jnp.einsum(
        "hqk,qhd->khd", probs_low, grad_attended, preferred_element_type=jnp.float32
    )
    grad_keys = (
        jnp.einsum("hqk,qhd->khd", scores_low, queries, preferred_element_type=jnp.float32)
        * score_scale
    )
    kv_grad = jnp.stack(
        (grad_keys.reshape(group_len, feat_local), grad_values.reshape(group_len, feat_local)),
        axis=1,
    )
    kv_mine, grad_up_part, grad_down_part = (
        lax.psum_scatter(
            kv_grad.astype(jnp.bfloat16), "ctx", scatter_dimension=0, tiled=True
        ).astype(jnp.float32),
        lax.psum_scatter(
            grad_up_local.astype(jnp.bfloat16), "ctx", scatter_dimension=1, tiled=True
        ).astype(jnp.float32),
        lax.psum_scatter(
            grad_down_local.astype(jnp.bfloat16), "ctx", scatter_dimension=2, tiled=True
        ).astype(jnp.float32),
    )
    project_grad = jnp.concatenate(
        (grad_queries.reshape(tok_count, 1, feat_local), kv_mine.astype(jnp.bfloat16)), axis=1
    )
    grad_normed_one = lax.psum(
        jnp.einsum(
            "tcf,dcf->td", project_grad, qkv_weight, preferred_element_type=jnp.float32
        ).astype(jnp.bfloat16),
        "tp",
    ).astype(jnp.float32)
    grad_qkv_local = jnp.einsum(
        "td,tcf->dcf", normed_low, project_grad, preferred_element_type=jnp.float32
    )
    grad_from_one, gain_one_grad = norm_backward(grad_normed_one, gain_one, normal_one, inverse_one)
    grad_input = grad_middle + grad_from_one
    summed_grads = (
        lax.psum_scatter(
            gain_one_grad.astype(jnp.bfloat16), "fsdp", scatter_dimension=0, tiled=True
        ).astype(jnp.float32),
        lax.psum_scatter(
            grad_qkv_local.astype(jnp.bfloat16), "fsdp", scatter_dimension=0, tiled=True
        ).astype(jnp.float32),
        lax.psum_scatter(
            grad_out_weight.astype(jnp.bfloat16), "fsdp", scatter_dimension=1, tiled=True
        ).astype(jnp.float32),
        lax.psum_scatter(
            bias_grad.astype(jnp.bfloat16), "fsdp", scatter_dimension=0, tiled=True
        ).astype(jnp.float32),
        lax.psum_scatter(
            gain_two_grad.astype(jnp.bfloat16), "fsdp", scatter_dimension=0, tiled=True
        ).astype(jnp.float32),
    )
    summed_grads = (
        lax.psum(summed_grads[0].astype(jnp.bfloat16), "ctx").astype(jnp.float32),
        lax.psum(summed_grads[1].astype(jnp.bfloat16), "ctx").astype(jnp.float32),
        lax.psum(summed_grads[2].astype(jnp.bfloat16), "ctx").astype(jnp.float32),
        lax.psum(summed_grads[3].astype(jnp.bfloat16), "ctx").astype(jnp.float32),
        lax.psum(summed_grads[4].astype(jnp.bfloat16), "ctx").astype(jnp.float32),
    )
    return (
        output,
        grad_input,
        summed_grads[0],
        summed_grads[1],
        summed_grads[2],
        summed_grads[3],
        summed_grads[4],
        grad_up_part,
        grad_down_part,
    )


def solution(mesh):
    in_specs = (
        P(("fsdp", "ctx"), None),
        P("fsdp"),
        P("fsdp", None, "tp"),
        P("tp", "fsdp"),
        P("fsdp", "tp"),
        P("fsdp"),
        P("fsdp", "ctx", "tp"),
        P("fsdp", "tp", "ctx"),
        P(("fsdp", "ctx"), None),
        P(("fsdp", "ctx"), None),
        P("fsdp", None),
        P(),
        P(("fsdp", "ctx"), None),
    )
    out_specs = (
        P(("fsdp", "ctx"), None),
        P(("fsdp", "ctx"), None),
        P("fsdp"),
        P("fsdp", None, "tp"),
        P("tp", "fsdp"),
        P("fsdp", "tp"),
        P("fsdp"),
        P("fsdp", "ctx", "tp"),
        P("fsdp", "tp", "ctx"),
    )
    return jax.shard_map(body, mesh=mesh, in_specs=in_specs, out_specs=out_specs, check_vma=False)
```

profile of v0, /device:TPU:0, one launch (start us, length us, event | category | flops | bytes accessed | tf_op | source)
XLA Modules:
  0.0 1017.3 jit_solution(10816884690926488151)
XLA Ops:
  12.5 18.5 %all-reduce.7 = (bf16[768]{0:T(1024)(128)(2,1)S(1)}, bf16[768]{0:T(1024)(128)(2,1)S(1)}) all-reduce(bf16[768]{0:T(1024)(128)(2,1)S(1)} %dynamic-update-slice, bf16[768]{0:T(1024)(128)(2,1)S(1)} %dynamic-update-slice.1), channel_id=1, replica_groups=mesh['fsdp'=8,'ctx'=2,'tp'=2] {'fsdp'}, use_global_device_ids=true, to_apply=%add.1 | all-reduce | flops 1536 | bytes 6144
  69.2 16.5 %all_gather.28 = bf16[384,768]{0,1:T(8,128)(2,1)} all-gather(bf16[384,96]{0,1:T(8,128)(2,1)S(1)} %copy-done.31), channel_id=1, replica_groups=mesh['fsdp'=8,'ctx'=2,'tp'=2] {'fsdp'}, dimensions={1}, use_global_device_ids=true | all-gather | bytes 663552 | tf_op jit(solution)/shard_map/all_gather | solution.py:92
  85.6 18.3 %fusion.2 = f32[576,1152,6]{1,2,0:T(8,128)} fusion(bf16[32,6,1]{1,0,2:T(8,128)(2,1)S(1)} %bitcast.134, s32[576,1152]{1,0:T(8,128)} %slice.49), kind=kOutput, calls=%fused_computation.5 | convolution fusion | flops 276037632 | bytes 18579840 | tf_op jit(solution)/shard_map/qkb,bh->hqk/dot_general | solution.py:63
  111.4 17.0 %fusion.7 = f32[6,576,1152]{2,1,0:T(8,128)} fusion(bf16[576,6,64]{0,2,1:T(8,128)(2,1)S(1)} %bitcast.119, bf16[1152,6,64]{0,2,1:T(8,128)(2,1)S(1)} %bitcast.117, f32[576,1152,6]{1,2,0:T(8,128)} %fusion.2, pred[576,1152]{1,0:T(8,128)(4,1)S(1)} %fusion.32), kind=kOutput, calls=%fused_computation.13 | convolution fusion | flops 521551872 | bytes 33841152 | tf_op jit(solution)/shard_map/qhd,khd->hqk/dot_general | solution.py:118
  128.4 17.3 %fusion.77 = (f32[6,576]{1,0:T(8,128)S(1)}, f32[6,576,1152]{2,1,0:T(8,128)}) fusion(f32[6,576,1152]{2,1,0:T(8,128)} %fusion.7), kind=kOutput, calls=%fused_computation.135 | output fusion | flops 7963775 | bytes 31864320 | tf_op jit(solution)/shard_map/sub | solution.py:124
  145.7 17.5 %fusion.48 = bf16[6,64,576]{2,1,0:T(8,128)(2,1)S(1)} fusion(bf16[1152,6,64]{0,2,1:T(8,128)(2,1)} %bitcast.129, f32[6,576]{1,0:T(8,128)S(1)} %get-tuple-element.33, f32[6,576,1152]{2,1,0:T(8,128)} %fusion.7), kind=kOutput, calls=%fused_computation.88 | convolution fusion | flops 521777664 | bytes 17266176 | tf_op jit(solution)/shard_map/hqk,khd->qhd/dot_general | solution.py:128
  168.3 32.9 %all-reduce.16.cloned.1.call-done = bf16[576,768]{1,0:T(8,128)(2,1)} async-done(((bf16[576,768]{1,0:T(8,128)(2,1)}), bf16[576,768]{1,0:T(8,128)(2,1)}) %all-reduce.16.cloned.1.call-update) | async-done | bytes 884752 | tf_op jit(solution)/shard_map/psum | solution.py:130
  229.5 64.1 %all-to-all-done = bf16[8,288,768]{2,1,0:T(8,128)(2,1)} async-done(((bf16[8,288,768]{2,1,0:T(8,128)(2,1)}), bf16[8,288,768]{2,1,0:T(8,128)(2,1)}, u32[]{:S(2)}, u32[]{:S(2)}) %all-to-all-start) | async-done | bytes 3538976 | tf_op jit(solution)/shard_map/all_to_all | solution.py:154
  299.4 37.4 %all-gather.10.cloned.1.call-done = bf16[1,768,1536]{2,1,0:T(8,128)(2,1)} async-done(((bf16[1,384,1536]{2,1,0:T(8,128)(2,1)}), bf16[1,768,1536]{2,1,0:T(8,128)(2,1)}) %all-gather.10.cloned.1.call-update) | async-done | bytes 2359312 | tf_op jit(solution)/shard_map/all_gather | solution.py:163
  348.0 26.3 %all-gather.12.cloned.1.call-done = bf16[1,1536,768]{2,1,0:T(8,128)(2,1)} async-done(((bf16[1,1536,384]{2,1,0:T(8,128)(2,1)}), bf16[1,1536,768]{2,1,0:T(8,128)(2,1)}) %all-gather.12.cloned.1.call-update) | async-done | bytes 2359312 | tf_op jit(solution)/shard_map/all_gather | solution.py:164
  378.1 17.2 %fusion.15 = bf16[2304,1536]{1,0:T(8,128)(2,1)S(1)} fusion(f32[2304,1536]{1,0:T(8,128)} %fusion.36, bf16[2304,768]{1,0:T(8,128)(2,1)} %bitcast.21, bf16[1,1536,768]{2,1,0:T(8,128)(2,1)} %all-gather.12.cloned.1.call-done), kind=kOutput, calls=%fused_computation.23 | convolution fusion | flops 5506596864 | bytes 27131904 | tf_op jit(solution)/shard_map/erd,efd->erf/dot_general | solution.py:191
  402.6 92.4 %all-reduce.18.cloned.1.call-done = bf16[8,288,768]{2,1,0:T(8,128)(2,1)} async-done(((bf16[8,288,768]{2,1,0:T(8,128)(2,1)}), bf16[8,288,768]{2,1,0:T(8,128)(2,1)}) %all-reduce.18.cloned.1.call-update) | async-done | bytes 3538960 | tf_op jit(solution)/shard_map/psum | solution.py:205
  495.0 85.1 %all_to_all.20 = bf16[8,288,768]{2,1,0:T(8,128)(2,1)S(1)} all-to-all(bf16[8,288,768]{2,1,0:T(8,128)(2,1)} %all-reduce.18.cloned.1.call-done), channel_id=1, replica_groups=mesh['fsdp'=8,'ctx'=2,'tp'=2] {'fsdp'}, dimensions={0} | all-to-all | bytes 7077888 | tf_op jit(solution)/shard_map/all_to_all | solution.py:206
  585.2 17.1 %fusion.25 = bf16[6,64,1152]{2,1,0:T(8,128)(2,1)S(1)} fusion(bf16[576,6,64]{0,2,1:T(8,128)(2,1)S(1)} %bitcast.132, f32[6,576]{1,0:T(8,128)S(1)} %copy-done.30, f32[6,576,1152]{2,1,0:T(8,128)} %fusion.7), kind=kOutput, calls=%fused_computation.47 | convolution fusion | flops 521998848 | bytes 17266176 | tf_op jit(solution)/shard_map/hqk,qhd->khd/dot_general | solution.py:234
  603.6 14.9 %multiply_reduce_fusion = (f32[6,576]{1,0:T(8,128)S(1)}, f32[6,576,1152]{2,1,0:T(8,128)}) fusion(f32[6,576,1152]{2,1,0:T(8,128)} %get-tuple-element.34, f32[6,576]{1,0:T(8,128)S(1)} %copy-done.30, bf16[576,6,64]{0,2,1:T(8,128)(2,1)} %bitcast.133, bf16[1152,6,64]{0,2,1:T(8,128)(2,1)} %bitcast.130), kind=kOutput, calls=%fused_computation.16 | convolution fusion | flops 521548416 | bytes 33205248 | tf_op jit(solution)/shard_map/qhd,khd->hqk/dot_general | solution.py:223
  632.7 13.6 %convolution_convert_fusion.1 = bf16[2304,768]{1,0:T(8,128)(2,1)} fusion(bf16[1,1536,768]{2,1,0:T(8,128)(2,1)} %all-gather.12.cloned.1.call-done, f32[2304,1536]{1,0:T(8,128)} %fusion.36), kind=kOutput, calls=%fused_computation.34 | convolution fusion | flops 5469437952 | bytes 20054016 | tf_op jit(solution)/shard_map/erf,efd->erd/dot_general | solution.py:168
  663.1 12.2 %fusion.23 = bf16[1,1536,768]{2,1,0:T(8,128)(2,1)} fusion(bf16[2304,768]{1,0:T(8,128)(2,1)} %bitcast.21, f32[2304,1536]{1,0:T(8,128)} %fusion.36), kind=kOutput, calls=%fused_computation.45 | convolution fusion | flops 5468848128 | bytes 20054016 | tf_op jit(solution)/shard_map/erf,erd->efd/dot_general | solution.py:196
  708.2 68.1 %all-reduce.20.cloned.1.call-done = (bf16[8,288,768]{2,1,0:T(8,128)(2,1)}, bf16[576,768]{1,0:T(8,128)(2,1)}) async-done(((bf16[8,288,768]{2,1,0:T(8,128)(2,1)}, bf16[576,768]{1,0:T(8,128)(2,1)}), (bf16[8,288,768]{2,1,0:T(8,128)(2,1)}, bf16[576,768]{1,0:T(8,128)(2,1)})) %all-reduce.20.cloned.1.call-update) | async-done | bytes 4423696 | tf_op jit(solution)/shard_map/psum | solution.py:171
  785.0 29.0 %reduce-scatter.16.cloned.1.call-done = bf16[384,1536]{1,0:T(8,128)(2,1)} async-done(((bf16[768,1536]{1,0:T(8,128)(2,1)}), bf16[384,1536]{1,0:T(8,128)(2,1)}) %reduce-scatter.16.cloned.1.call-update) | async-done | bytes 1179664
  827.2 24.2 %reduce-scatter.14.cloned.1.call-done = bf16[1,384,1536]{2,1,0:T(8,128)(2,1)} async-done(((bf16[1,768,1536]{2,1,0:T(8,128)(2,1)}), bf16[1,384,1536]{2,1,0:T(8,128)(2,1)}) %reduce-scatter.14.cloned.1.call-update) | async-done | bytes 1179664 | tf_op jit(solution)/shard_map/reduce_scatter | solution.py:249
  854.4 30.5 %reduce-scatter.12.cloned.1.call-done = bf16[384,96]{0,1:T(8,128)(2,1)} async-done(((bf16[384,768]{0,1:T(8,128)(2,1)}), bf16[384,96]{0,1:T(8,128)(2,1)}) %reduce-scatter.12.cloned.1.call-update) | async-done | bytes 73744 | tf_op jit(solution)/shard_map/reduce_scatter | solution.py:277
  884.9 35.7 %reduce-scatter.10.cloned.1.call-done = bf16[96,3,384]{2,0,1:T(8,128)(2,1)} async-done(((bf16[768,3,384]{2,0,1:T(8,128)(2,1)}), bf16[96,3,384]{2,0,1:T(8,128)(2,1)}) %reduce-scatter.10.cloned.1.call-update) | async-done | bytes 221200 | tf_op jit(solution)/shard_map/reduce_scatter | solution.py:274
  920.7 16.5 %fusion.54 = bf16[32,6]{1,0:T(8,128)(2,1)} fusion(bf16[6,576,1152]{2,1,0:T(8,128)(2,1)} %copy-done.1, s32[576,1152]{1,0:T(8,128)} %slice.49), kind=kOutput, calls=%fused_computation.91 | convolution fusion | flops 276037824 | bytes 10617216 | tf_op jit(solution)/shard_map/hqk,qkb->bh/dot_general | solution.py:233
  951.2 28.1 %all-reduce.6 = (bf16[768]{0:T(1024)(128)(2,1)}, bf16[32,6]{1,0:T(8,128)(2,1)}, bf16[768]{0:T(1024)(128)(2,1)}) all-reduce(bf16[768]{0:T(1024)(128)(2,1)} %get-tuple-element.11, bf16[32,6]{1,0:T(8,128)(2,1)} %fusion.54, bf16[768]{0:T(1024)(128)(2,1)} %get-tuple-element.9), channel_id=3, replica_groups=mesh['fsdp'=8,'ctx'=2,'tp'=2] {'fsdp'}, use_global_device_ids=true, to_apply=%region_23.24.clone | all-reduce | flops 1728 | bytes 6912
  (227 shorter events, 249.9 us)
Async XLA Ops:
  7.2 57.0 %all-gather.6.cloned.1.call-start = ((), (), s32[]{:S(2)}) async-start(), calls=%async_computation.9 | async-start | bytes 1990656 | tf_op jit(solution)/shard_map/all_gather | solution.py:91
  7.9 96.3 %all-gather.8.cloned.1.call-start = ((), (), s32[]{:S(2)}) async-start(), calls=%async_computation.10 | async-start | bytes 2654208 | tf_op jit(solution)/shard_map/all_gather | solution.py:107
  30.9 33.2 %copy-start.32 = (f32[768]{0:T(1024)}, f32[768]{0:T(1024)S(1)}, u32[]{:S(2)}) copy-start(f32[768]{0:T(1024)S(1)} %convert_element_type.163) | copy-start | bytes 9220
  69.1 132.0 %all-reduce.16.cloned.1.call-start = ((), (), s32[]{:S(2)}) async-start(), calls=%async_computation.11 | async-start | bytes 1769472 | tf_op jit(solution)/shard_map/psum | solution.py:130
  108.8 19.6 %copy-start.8 = (bf16[1152,1,384]{0,2,1:T(8,128)(2,1)}, bf16[1152,1,384]{0,2,1:T(8,128)(2,1)S(1)}, u32[]{:S(2)}) copy-start(bf16[1152,1,384]{0,2,1:T(8,128)(2,1)S(1)} %copy.70) | copy-start | bytes 2654212
  163.2 39.4 %copy-start.20 = (bf16[6,64,576]{2,1,0:T(8,128)(2,1)}, bf16[6,64,576]{2,1,0:T(8,128)(2,1)S(1)}, u32[]{:S(2)}) copy-start(bf16[6,64,576]{2,1,0:T(8,128)(2,1)S(1)} %fusion.48) | copy-start | bytes 1327108
  165.7 48.3 %copy-start.27 = (s32[1152]{0:T(1024)}, s32[1152]{0:T(1024)S(1)}, u32[]{:S(2)}) copy-start(s32[1152]{0:T(1024)S(1)} %fusion.66) | copy-start | bytes 13828
  168.3 40.6 %copy-start.23 = (pred[2304,576]{0,1:T(8,128)(4,1)}, pred[2304,576]{0,1:T(8,128)(4,1)S(1)}, u32[]{:S(2)}) copy-start(pred[2304,576]{0,1:T(8,128)(4,1)S(1)} %fusion.17) | copy-start | bytes 3981316
  208.9 84.8 %all-to-all-start = ((bf16[8,288,768]{2,1,0:T(8,128)(2,1)}), bf16[8,288,768]{2,1,0:T(8,128)(2,1)}, u32[]{:S(2)}, u32[]{:S(2)}) async-start(bf16[8,288,768]{2,1,0:T(8,128)(2,1)} %bitcast.122), calls=%async_computation | async-start | bytes 7077888 | tf_op jit(solution)/shard_map/all_to_all | solution.py:154
  293.7 84.5 %all-to-all-start.2 = ((bf16[8,288,768]{2,1,0:T(8,128)(2,1)}), bf16[8,288,768]{2,1,0:T(8,128)(2,1)}, u32[]{:S(2)}, u32[]{:S(2)}) async-start(bf16[8,288,768]{2,1,0:T(8,128)(2,1)} %multiply_convert_fusion.2), calls=%async_computation.2 | async-start | bytes 7077888 | tf_op jit(solution)/shard_map/all_to_all | solution.py:183
  298.2 38.6 %all-gather.10.cloned.1.call-start = ((), (), s32[]{:S(2)}) async-start(), calls=%async_computation.12 | async-start | bytes 3538944 | tf_op jit(solution)/shard_map/all_gather | solution.py:163
  298.8 75.5 %all-gather.12.cloned.1.call-start = ((), (), s32[]{:S(2)}) async-start(), calls=%async_computation.13 | async-start | bytes 3538944 | tf_op jit(solution)/shard_map/all_gather | solution.py:164
  299.3 195.7 %all-reduce.18.cloned.1.call-start = ((), (), s32[]{:S(2)}) async-start(), calls=%async_computation.14 | async-start | bytes 7077888 | tf_op jit(solution)/shard_map/psum | solution.py:205
  402.6 177.6 %copy-start.10 = (bf16[576,768]{1,0:T(8,128)(2,1)S(1)}, bf16[576,768]{1,0:T(8,128)(2,1)}, u32[]{:S(2)}) copy-start(bf16[576,768]{1,0:T(8,128)(2,1)} %all-reduce.16.cloned.1.call-done) | copy-start | bytes 2654212
  402.6 256.4 %reduce-scatter.8.cloned.1.call-start = ((), (), s32[]{:S(2)}) async-start(), calls=%async_computation.15 | async-start | bytes 2654208 | tf_op jit(solution)/shard_map/reduce_scatter | solution.py:246
  495.0 85.1 %copy-start.24 = (pred[2304,576]{0,1:T(8,128)(4,1)S(1)}, pred[2304,576]{0,1:T(8,128)(4,1)}, u32[]{:S(2)}) copy-start(pred[2304,576]{0,1:T(8,128)(4,1)} %copy-done.23) | copy-start | bytes 3981316
  584.3 117.9 %copy-start.2 = (f32[576,768]{1,0:T(8,128)}, f32[576,768]{1,0:T(8,128)S(1)}, u32[]{:S(2)}) copy-start(f32[576,768]{1,0:T(8,128)S(1)} %multiply_add_fusion) | copy-start | bytes 5308420
  632.7 143.7 %all-reduce.20.cloned.1.call-start = ((), (), s32[]{:S(2)}) async-start(), calls=%async_computation.20 | async-start | bytes 8847360 | tf_op jit(solution)/shard_map/psum | solution.py:171
  663.0 150.9 %reduce-scatter.16.cloned.1.call-start = ((), (), s32[]{:S(2)}) async-start(), calls=%async_computation.19 | async-start | bytes 3538944
  691.8 159.7 %reduce-scatter.14.cloned.1.call-start = ((), (), s32[]{:S(2)}) async-start(), calls=%async_computation.18 | async-start | bytes 3538944 | tf_op jit(solution)/shard_map/reduce_scatter | solution.py:249
  702.1 182.8 %reduce-scatter.12.cloned.1.call-start = ((), (), s32[]{:S(2)}) async-start(), calls=%async_computation.17 | async-start | bytes 663552 | tf_op jit(solution)/shard_map/reduce_scatter | solution.py:277
  703.9 216.8 %reduce-scatter.10.cloned.1.call-start = ((), (), s32[]{:S(2)}) async-start(), calls=%async_computation.16 | async-start | bytes 1990656 | tf_op jit(solution)/shard_map/reduce_scatter | solution.py:274
  776.4 217.0 %all-to-all-start.1 = ((bf16[8,288,768]{2,1,0:T(8,128)(2,1)}), bf16[8,288,768]{2,1,0:T(8,128)(2,1)S(1)}, u32[]{:S(2)}, u32[]{:S(2)}) async-start(bf16[8,288,768]{2,1,0:T(8,128)(2,1)} %get-tuple-element.18), calls=%async_computation.1 | async-start | bytes 7077888 | tf_op jit(solution)/shard_map/all_to_all | solution.py:172
  781.1 164.0 %all-reduce.22.cloned.1.call-start = ((), (), s32[]{:S(2)}) async-start(), calls=%async_computation.21 | async-start | bytes 589824 | tf_op jit(solution)/shard_map/psum | solution.py:289
  (38 other events, 310.2 us)
Sparse Core Ops, SparseCore 0:
  9.6 29.2 all-gather.5
  69.2 29.0 all-gather.7
  165.0 36.1 all-reduce.15
  300.3 36.4 all-gather.9
  338.1 36.0 all-gather.11
  402.7 92.2 all-reduce.17
  632.8 26.1 reduce-scatter.7
  663.1 113.1 all-reduce.19
  779.2 34.7 reduce-scatter.15
  816.7 34.6 reduce-scatter.13
  853.7 31.1 reduce-scatter.11
  887.6 32.9 reduce-scatter.9
  923.0 22.0 all-reduce.21
where the time goes:
time: 1030 us; the launch traced here: 1020 us
  waiting for transfers between devices  461 us (45%)
  matrix products  204 us (20%)
  blocking collectives  162 us (16%)
  local copies, waits for them, and re-layouts  89.3 us (9%)
  other arithmetic  68.9 us (7%)
  between operations  17 us (2%)
  starting transfers between devices  14.5 us (1%)
    psum x1, waiting for transfers between devices, body(): row_grad = lax.psum(row_grad_part.astype(jnp.bfloat16), 'tp')  92.4 us
    all_to_all x1, blocking collectives, body(): lax.all_to_all(from_experts(row_grad, fsdp_size, exp_dev, capacity, width...  85.1 us
    psum x1, waiting for transfers between devices, body(): expert_out = lax.psum(partial_out.astype(jnp.bfloat16), 'tp')  68.1 us
    all_to_all x1, waiting for transfers between devices, body(): lax.all_to_all(send_rows.reshape(fsdp_size, exp_dev * capacity, width), '...  64.1 us
    unnamed x2, blocking collectives  46.5 us
    unnamed x104, local copies, waits for them, and re-layouts  37.9 us
    all_gather x1, waiting for transfers between devices, body(): lax.all_gather(w_up, 'ctx', axis=1, tiled=True)  37.4 us
    reduce_scatter x1, waiting for transfers between devices, body(): lax.psum_scatter(grad_qkv_local.astype(jnp.bfloat16), 'fsdp', scatter_dim...  35.7 us
  transfers between devices with their start and end apart: 16, of which 13 were waited for; matrix products, arithmetic and copies ran while one was open for 19% of the time, Pallas kernels for 0%

commit v1 on v0

v1 whole, which is shorter than its diff:
```python
import functools

import jax
import jax.numpy as jnp
from jax import lax
from jax.experimental import pallas as pl
from jax.experimental.pallas import tpu as pltpu
from jax.sharding import PartitionSpec as P

HEAD_DIM = 64
TOP = 2
LANES = 128
eps = 1e-06
F32 = jnp.float32
BF16 = jnp.bfloat16
SCALE = HEAD_DIM ** (-0.5)
VMEM = 48 * 1024 * 1024


def dot(a, b, dims=((1,), (0,))):
    return lax.dot_general(a, b, (dims, ((), ())), preferred_element_type=F32)


NT = ((1,), (1,))
TN = ((0,), (0,))


def norm_forward(values, gain_vec):
    inverse = lax.rsqrt(jnp.mean(values * values, axis=-1, keepdims=True) + eps)
    normal = values * inverse
    return (normal * gain_vec, normal, inverse)


def norm_backward(upstream, gain_vec, normal, inverse):
    gain_grad = jnp.sum(upstream * normal, axis=0)
    scaled = upstream * gain_vec
    input_grad = inverse * (scaled - normal * jnp.mean(scaled * normal, axis=-1, keepdims=True))
    return (input_grad, gain_grad)


def round_low(x):
    return lax.reduce_precision(x.astype(F32), 8, 7).astype(BF16)


def swap(x, axis):
    return lax.ppermute(x, axis, [(0, 1), (1, 0)])


def in_order(mine, other, index, axis):
    return jnp.where(
        index == 0,
        jnp.concatenate((mine, other), axis=axis),
        jnp.concatenate((other, mine), axis=axis),
    )


def gather_axis(x, name, axis):
    if lax.axis_size(name) == 2:
        return in_order(x, swap(x, name), lax.axis_index(name), axis)
    return lax.all_gather(x, name, axis=axis, tiled=True)


def scatter_axis(x, name, axis):
    if lax.axis_size(name) == 2:
        size = x.shape[axis] // 2
        index = lax.axis_index(name)
        away = lax.dynamic_slice_in_dim(x, (1 - index) * size, size, axis)
        kept = lax.dynamic_slice_in_dim(x, index * size, size, axis)
        return kept.astype(F32) + swap(away.astype(BF16), name).astype(F32)
    return lax.psum_scatter(x.astype(BF16), name, scatter_dimension=axis, tiled=True).astype(F32)


def sum_axis(x, name):
    if lax.axis_size(name) == 2:
        return x.astype(F32) + swap(x, name).astype(F32)
    return lax.psum(x, name).astype(F32)


def sibling(x):
    size = lax.axis_size("fsdp")
    return lax.ppermute(x, "fsdp", [(i, i ^ 1) for i in range(size)])


def line(x, chips, step):
    perm = [(2 * c + k, 2 * (c + step) + k) for c in chips for k in range(2)]
    return lax.ppermute(x, "fsdp", perm)


def line_gather(x):
    chips = lax.axis_size("fsdp") // 2
    chip = lax.axis_index("fsdp") // 2
    below, above = [], []
    up, down = x, x
    for s in range(1, chips):
        up = line(up, range(s - 1, chips - 1), 1)
        down = line(down, range(1, chips - s + 1), -1)
        below.append(up)
        above.append(down)
    every = jnp.stack(below[::-1] + [x] + above)
    mine = lax.dynamic_slice_in_dim(every, chips - 1 - chip, chips, 0)
    return mine, sibling(mine)


def line_scatter(mine, other):
    chips = lax.axis_size("fsdp") // 2
    chip = lax.axis_index("fsdp") // 2
    part = (mine.astype(F32) + sibling(other).astype(F32)).astype(BF16)
    up = down = None
    for t in range(1, chips):
        high = lax.dynamic_index_in_dim(part, jnp.minimum(chip + chips - t, chips - 1), 0, False)
        low = lax.dynamic_index_in_dim(part, jnp.maximum(chip - chips + t, 0), 0, False)
        if up is not None:
            high = (high.astype(F32) + up.astype(F32)).astype(BF16)
            low = (low.astype(F32) + down.astype(F32)).astype(BF16)
        up = line(high, range(0, t), 1)
        down = line(low, range(chips - t, chips), -1)
    own = lax.dynamic_index_in_dim(part, chip, 0, False)
    return own.astype(F32) + (up.astype(F32) + down.astype(F32))


def by_index(mine, other):
    core = lax.axis_index("fsdp") % 2
    return jnp.where(
        core == 0, jnp.stack((mine, other), axis=1), jnp.stack((other, mine), axis=1)
    )


def by_core(blocks):
    core = lax.axis_index("fsdp") % 2
    pairs = blocks.reshape((blocks.shape[0] // 2, 2) + blocks.shape[1:])
    return (
        jnp.where(core == 0, pairs[:, 0], pairs[:, 1]),
        jnp.where(core == 0, pairs[:, 1], pairs[:, 0]),
    )


def half_lanes(x, h):
    lane = lax.broadcasted_iota(jnp.int32, x.shape, 1)
    return jnp.where((lane >= HEAD_DIM) == (h == 1), x, jnp.zeros_like(x))


def join_lanes(a, b):
    lane = lax.broadcasted_iota(jnp.int32, a.shape, 1)
    return jnp.where(lane < HEAD_DIM, a, b)


def attend_kernel(tile, q_ref, k_ref, v_ref, vec_ref, lo_ref, hi_ref, o_ref, p_ref):
    rows, keys = q_ref.shape[0], k_ref.shape[0]
    k, v = k_ref[...], v_ref[...]
    place = lax.broadcasted_iota(jnp.int32, (tile, keys), 1)
    for start in range(0, rows, tile):
        at = pl.ds(start, tile)
        q = q_ref[at, :]
        allowed = (place >= lo_ref[at, :]) & (place <= hi_ref[at, :])
        outs = []
        for h in range(2):
            bias = pltpu.roll(
                jnp.broadcast_to(vec_ref[0, h : h + 1, :], (tile, keys)),
                start,
                1,
                stride=1,
                stride_axis=0,
            )
            s = dot(half_lanes(q, h), k, NT) * SCALE + bias
            s = jnp.where(allowed, s, -1e30)
            e = jnp.exp(s - jnp.max(s, axis=1, keepdims=True))
            p = (e * (1.0 / jnp.sum(e, axis=1, keepdims=True))).astype(BF16)
            p_ref[h, at, :] = p
            outs.append(dot(p, v))
        o_ref[at, :] = join_lanes(*outs).astype(BF16)


def attend_back_kernel(tile, q_ref, k_ref, v_ref, p_ref, go_ref, dq_ref, dk_ref, dv_ref, diag_ref):
    rows, keys = q_ref.shape[0], k_ref.shape[0]
    k, v = k_ref[...], v_ref[...]
    dk = [jnp.zeros((keys, LANES), F32) for _ in range(2)]
    dv = [jnp.zeros((keys, LANES), F32) for _ in range(2)]
    diag = [jnp.zeros((8, keys), F32) for _ in range(2)]
    for start in range(0, rows, tile):
        at = pl.ds(start, tile)
        q, go = q_ref[at, :], go_ref[at, :]
        dq = []
        for h in range(2):
            p_low = p_ref[h, at, :]
            p = p_low.astype(F32)
            dp = dot(half_lanes(go, h), v, NT)
            ds = p * (dp - jnp.sum(p * dp, axis=1, keepdims=True))
            low = ds.astype(BF16)
            dq.append(dot(low, k))
            dk[h] = dk[h] + dot(low, q, TN)
            dv[h] = dv[h] + dot(p_low, go, TN)
            while ds.shape[0] % 16 == 0:
                n = ds.shape[0] // 2
                ds = ds[:n] + pltpu.roll(ds[n:], keys - n, 1)
            total = ds[:8]
            for g in range(8, ds.shape[0], 8):
                total = total + pltpu.roll(ds[g : g + 8], keys - g, 1)
            if start:
                total = pltpu.roll(total, keys - start, 1)
            diag[h] = diag[h] + total
        dq_ref[at, :] = (join_lanes(*dq) * SCALE).astype(BF16)
    dk_ref[...] = (join_lanes(*dk) * SCALE).astype(BF16)
    dv_ref[...] = join_lanes(*dv).astype(BF16)
    for h in range(2):
        diag_ref[0, h] = diag[h]


def row_tile(rows):
    return 192 if rows % 192 == 0 else rows


def attend(project, kv, vec, lo, hi):
    rows, keys = project.shape[0], kv.shape[0]
    pairs = kv.shape[1] // 2 // LANES
    column = lambda shift: lambda g: (0, g + shift)
    return pl.pallas_call(
        functools.partial(attend_kernel, row_tile(rows)),
        grid=(pairs,),
        in_specs=[
            pl.BlockSpec((rows, LANES), column(0)),
            pl.BlockSpec((keys, LANES), column(0)),
            pl.BlockSpec((keys, LANES), column(pairs)),
            pl.BlockSpec((1, 2, keys), lambda g: (g, 0, 0)),
            pl.BlockSpec((rows, 1), lambda g: (0, 0)),
            pl.BlockSpec((rows, 1), lambda g: (0, 0)),
        ],
        out_specs=[
            pl.BlockSpec((rows, LANES), column(0)),
            pl.BlockSpec((2, rows, keys), lambda g: (g, 0, 0)),
        ],
        out_shape=[
            jax.ShapeDtypeStruct((rows, pairs * LANES), BF16),
            jax.ShapeDtypeStruct((2 * pairs, rows, keys), BF16),
        ],
        compiler_params=pltpu.CompilerParams(vmem_limit_bytes=VMEM),
        cost_estimate=pl.CostEstimate(
            flops=8 * pairs * rows * keys * LANES,
            bytes_accessed=4 * pairs * rows * keys,
            transcendentals=2 * pairs * rows * keys,
        ),
        name="attend",
    )(project, kv, kv, vec.reshape(pairs, 2, keys), lo, hi)


def attend_back(project, kv, probs, go):
    rows, keys = project.shape[0], kv.shape[0]
    pairs = kv.shape[1] // 2 // LANES
    column = lambda shift: lambda g: (0, g + shift)
    return pl.pallas_call(
        functools.partial(attend_back_kernel, row_tile(rows)),
        grid=(pairs,),
        in_specs=[
            pl.BlockSpec((rows, LANES), column(0)),
            pl.BlockSpec((keys, LANES), column(0)),
            pl.BlockSpec((keys, LANES), column(pairs)),
            pl.BlockSpec((2, rows, keys), lambda g: (g, 0, 0)),
            pl.BlockSpec((rows, LANES), column(0)),
        ],
        out_specs=[
            pl.BlockSpec((rows, LANES), column(0)),
            pl.BlockSpec((keys, LANES), column(0)),
            pl.BlockSpec((keys, LANES), column(0)),
            pl.BlockSpec((1, 2, 8, keys), lambda g: (g, 0, 0, 0)),
        ],
        out_shape=[
            jax.ShapeDtypeStruct((rows, pairs * LANES), BF16),
            jax.ShapeDtypeStruct((keys, pairs * LANES), BF16),
            jax.ShapeDtypeStruct((keys, pairs * LANES), BF16),
            jax.ShapeDtypeStruct((pairs, 2, 8, keys), F32),
        ],
        compiler_params=pltpu.CompilerParams(vmem_limit_bytes=VMEM),
        cost_estimate=pl.CostEstimate(
            flops=16 * pairs * rows * keys * LANES,
            bytes_accessed=4 * pairs * rows * keys,
            transcendentals=0,
        ),
        name="attend_back",
    )(project, kv, kv, probs, go)


def expert(rows, grads, up, down):
    out = back = 0.0
    up_grad, down_grad = [], []
    for f in range(2):
        inner, pull = jax.vjp(jax.nn.gelu, dot(rows, up[f]))
        hidden = inner.astype(BF16)
        inner_grad = pull(dot(grads, down[f], NT))[0].astype(BF16)
        out = out + dot(hidden, down[f])
        back = back + dot(inner_grad, up[f], NT)
        up_grad.append(dot(rows, inner_grad, TN).astype(BF16))
        down_grad.append(dot(hidden, grads, TN).astype(BF16))
    return out.astype(BF16), back.astype(BF16), up_grad, down_grad


def body(
    tokens,
    norm1_gain,
    w_qkv,
    w_out,
    rel_bias,
    norm2_gain,
    w_up,
    w_down,
    gates,
    routes,
    lengths,
    buckets,
    grad_out,
):
    count, width = tokens.shape
    ctx_index, tp_index = lax.axis_index("ctx"), lax.axis_index("tp")
    ctx_size, fsdp_size = lax.axis_size("ctx"), lax.axis_size("fsdp")
    group_len = count * ctx_size
    half = count // 2
    feat = w_qkv.shape[2]
    heads = feat // HEAD_DIM
    share = w_qkv.shape[0]
    bias_rows = rel_bias.shape[0]
    buckets_all = bias_rows * fsdp_size
    mine = lambda x: lax.dynamic_slice_in_dim(x, tp_index * half, half, 0)

    small = jnp.zeros((share, LANES), BF16)
    small = small.at[:, 0].set(norm1_gain).at[:, 1].set(norm2_gain)
    small = small.at[:bias_rows, 2 : 2 + heads].set(rel_bias)
    packed = jnp.concatenate((w_qkv.reshape(share, 3 * feat), w_out.T, small), axis=1)
    packed = by_index(*line_gather(packed)).reshape(fsdp_size * share, packed.shape[1])
    qkv_weight = packed[:, : 3 * feat]
    out_weight = packed[:, 3 * feat : 4 * feat]
    small = packed[:, 4 * feat :]
    gain_one, gain_two = small[:, 0].astype(F32), small[:, 1].astype(F32)
    table = small[:, 2 : 2 + heads].reshape(fsdp_size, share, heads)[:, :bias_rows]
    table = table.reshape(buckets_all, heads)

    up_mine = gather_axis(w_up[0], "ctx", 0)
    up = (up_mine, swap(up_mine, "tp"))
    down = jnp.concatenate((w_down[0], swap(w_down[0], "tp")), axis=0)
    down = gather_axis(down, "ctx", 1)
    hidden = w_down.shape[1]
    down = (down[:hidden], down[hidden:])

    extra = jnp.concatenate((routes.astype(BF16), gates.astype(BF16)), axis=1)
    extra = jnp.pad(extra, ((0, 0), (0, LANES - 2 * TOP)))
    told = mine(jnp.concatenate((grad_out.astype(BF16), extra), axis=1))

    inputs = tokens.astype(F32)
    normed_low = norm_forward(inputs, gain_one)[0].astype(BF16)
    project = dot(normed_low, qkv_weight).astype(BF16)
    kv = gather_axis(project[:, feat:], "ctx", 0)
    start = ctx_index * count
    hi = start + jnp.arange(count, dtype=jnp.int32)
    ends = jnp.cumsum(lengths[0])
    lo = jnp.max(jnp.where(hi[:, None] >= ends[None, :], ends[None, :], 0), axis=1)
    flipped = buckets[::-1]
    turned = lax.dynamic_slice_in_dim(
        jnp.concatenate((flipped, flipped)), group_len - 1 - start, group_len
    )
    hot = (turned[None, :] == jnp.arange(buckets_all, dtype=jnp.int32)[:, None]).astype(BF16)
    vec = dot(table, hot, TN)
    attended, probs = attend(project, kv, vec, lo[:, None], hi[:, None])
    branch = dot(attended, out_weight, NT).astype(BF16)
    middle = mine(inputs) + scatter_axis(branch, "tp", 0)
    normed_two, normal_two, inverse_two = norm_forward(middle, gain_two)

    told = jnp.concatenate(line_gather(told), axis=0).reshape(fsdp_size * half, -1)
    rows = jnp.concatenate(line_gather(normed_two.astype(BF16)), axis=0)
    rows = rows.reshape(fsdp_size * half, width)
    expert_index = lax.axis_index("fsdp").astype(F32)
    named = told[:, width : width + TOP].astype(F32) == expert_index
    gate = jnp.where(named, told[:, width + TOP : width + 2 * TOP].astype(F32), 0.0)
    gate = jnp.sum(gate, axis=1, keepdims=True)
    grads = (gate * told[:, :width].astype(F32)).astype(BF16)
    chosen = jnp.any(named, axis=1)
    order = jnp.cumsum(chosen.astype(jnp.int32)) - 1
    total = rows.shape[0]
    room = -(-(4 * TOP * total) // (3 * fsdp_size * LANES)) * LANES
    room = min(room, total)

    def few(rows, grads, order, chosen):
        pick = (
            (order[None, :] == jnp.arange(room, dtype=jnp.int32)[:, None]) & chosen[None, :]
        ).astype(BF16)
        out, back, up_grad, down_grad = expert(
            dot(pick, rows).astype(BF16), dot(pick, grads).astype(BF16), up, down
        )
        spread = lambda x: dot(pick, x, TN).astype(BF16)
        return spread(out), spread(back), up_grad, down_grad

    def many(rows, grads, order, chosen):
        return expert(rows, grads, up, down)

    expert_out, row_grad, up_grad, down_grad = lax.cond(
        jnp.sum(chosen.astype(jnp.int32)) <= room, few, many, rows, grads, order, chosen
    )
    row_grad = jnp.where(chosen[:, None], row_grad, jnp.zeros_like(row_grad))
    expert_out = (gate * expert_out.astype(F32)).astype(BF16)
    lines = lambda x: x.reshape(2, fsdp_size // 2, half, width)
    row_grad, expert_out = lines(row_grad), lines(expert_out)
    grad_normed_two = line_scatter(row_grad[0], row_grad[1])
    mixture = line_scatter(expert_out[0], expert_out[1])
    output = gather_axis(round_low(middle + mixture), "tp", 0).astype(F32)

    up_sum = up_grad[0].astype(F32) + swap(up_grad[1], "tp").astype(F32)
    grad_up = scatter_axis(up_sum, "ctx", 0)[None]
    down_sum = scatter_axis(jnp.stack(down_grad), "ctx", 2)
    grad_down = (down_sum[0] + swap(down_sum[1].astype(BF16), "tp").astype(F32))[None]

    grad_from_two, gain_two_grad = norm_backward(grad_normed_two, gain_two, normal_two, inverse_two)
    grad_middle = mine(grad_out) + grad_from_two
    grad_branch = gather_axis(grad_middle.astype(BF16), "tp", 0)
    grad_attended = dot(grad_branch, out_weight).astype(BF16)
    grad_q, grad_k, grad_v, diag = attend_back(project, kv, probs, grad_attended)
    grad_out_weight = dot(grad_branch, attended, TN)
    kv_mine = scatter_axis(jnp.concatenate((grad_k, grad_v), axis=1), "ctx", 0)
    project_grad = jnp.concatenate((grad_q, kv_mine.astype(BF16)), axis=1)
    grad_normed_one = scatter_axis(dot(project_grad, qkv_weight, NT).astype(BF16), "tp", 0)
    grad_qkv = dot(normed_low, project_grad, TN)
    _, normal_one, inverse_one = norm_forward(mine(inputs), gain_one)
    grad_from_one, gain_one_grad = norm_backward(grad_normed_one, gain_one, normal_one, inverse_one)
    grad_input = gather_axis(round_low(grad_middle + grad_from_one), "tp", 0).astype(F32)

    diag = diag.reshape(heads, 8, group_len)
    diag = sum(jnp.roll(diag[:, r], -r, axis=1) for r in range(8))
    bias_grad = lax.dot_general(
        hot.astype(F32), diag, (NT, ((), ())), precision=lax.Precision.HIGHEST
    )
    gain_grads = jnp.stack((gain_one_grad, gain_two_grad), axis=1)
    gain_grads = gain_grads + swap(gain_grads, "tp")
    bias_grad = bias_grad.reshape(fsdp_size, bias_rows, heads)
    bias_grad = jnp.pad(bias_grad, ((0, 0), (0, share - bias_rows), (0, 0)))
    small = jnp.concatenate((gain_grads, bias_grad.reshape(-1, heads)), axis=1)
    small = jnp.pad(small, ((0, 0), (0, LANES - 2 - heads)))
    packed = jnp.concatenate(
        (grad_qkv.astype(BF16), grad_out_weight.astype(BF16), small.astype(BF16)), axis=1
    ).reshape(fsdp_size, share, -1)
    packed = sum_axis(round_low(line_scatter(*by_core(packed))), "ctx")
    return (
        output,
        grad_input,
        packed[:, 4 * feat],
        packed[:, : 3 * feat].reshape(share, 3, feat),
        packed[:, 3 * feat : 4 * feat].T,
        packed[:bias_rows, 4 * feat + 2 : 4 * feat + 2 + heads],
        packed[:, 4 * feat + 1],
        grad_up,
        grad_down,
    )


def solution(mesh):
    in_specs = (
        P(("fsdp", "ctx"), None),
        P("fsdp"),
        P("fsdp", None, "tp"),
        P("tp", "fsdp"),
        P("fsdp", "tp"),
        P("fsdp"),
        P("fsdp", "ctx", "tp"),
        P("fsdp", "tp", "ctx"),
        P(("fsdp", "ctx"), None),
        P(("fsdp", "ctx"), None),
        P("fsdp", None),
        P(),
        P(("fsdp", "ctx"), None),
    )
    out_specs = (
        P(("fsdp", "ctx"), None),
        P(("fsdp", "ctx"), None),
        P("fsdp"),
        P("fsdp", None, "tp"),
        P("tp", "fsdp"),
        P("fsdp", "tp"),
        P("fsdp"),
        P("fsdp", "ctx", "tp"),
        P("fsdp", "tp", "ctx"),
    )
    return jax.shard_map(body, mesh=mesh, in_specs=in_specs, out_specs=out_specs, check_vma=False)
```

time: 1030 us -> 736 us (0.71); the launches traced: 1020 us -> 738 us
  waiting for transfers between devices: 461 us -> 255 us
  starting transfers between devices: 14.5 us -> 200 us
  blocking collectives: 162 us -> 0 us
  matrix products: 204 us -> 92.5 us
  local copies, waits for them, and re-layouts: 89.3 us -> 47.3 us
  Pallas kernels: 0 us -> 39.3 us
  other arithmetic: 68.9 us -> 94.3 us
  between operations: 17 us -> 3.21 us
    ppermute x0 -> x59, waiting for transfers between devices: none -> 255 us  [the longest x17 161 us: swap(): return lax.ppermute(x, axis, [(0, 1), (1, 0)])]
    psum x4 -> x0, waiting for transfers between devices: 201 us -> none  [the longest x1 92.4 us: body(): row_grad = lax.psum(row_grad_part.astype(jnp.bfloat16), 'tp')]
    ppermute x0 -> x59, starting transfers between devices: none -> 200 us  [the longest x36 178 us: line(): return lax.ppermute(x, 'fsdp', perm)]
    dot_general x22, matrix products: 204 us -> 92.5 us  [the longest x21 91.6 us: dot(): return lax.dot_general(a, b, (dims, ((), ())), preferred_element_type=F32)]
    reduce_scatter x4 -> x0, waiting for transfers between devices: 97.1 us -> none  [the longest x1 35.7 us: body(): lax.psum_scatter(grad_qkv_local.astype(jnp.bfloat16), 'fsdp', scatter_dim...]
    all_to_all x1 -> x0, blocking collectives: 85.1 us -> none  [body(): lax.all_to_all(from_experts(row_grad, fsdp_size, exp_dev, capacity, width...]
    all_to_all x3 -> x0, waiting for transfers between devices: 68 us -> none  [the longest x1 64.1 us: body(): lax.all_to_all(send_rows.reshape(fsdp_size, exp_dev * capacity, width), '...]
    all_gather x4 -> x0, waiting for transfers between devices: 63.7 us -> none  [the longest x1 37.4 us: body(): lax.all_gather(w_up, 'ctx', axis=1, tiled=True)]
  transfers between devices with their start and end apart: 16 -> 59, of which waited for: 13 -> 27; matrix products, arithmetic and copies ran while one was open for 19% -> 17% of each run, Pallas kernels for 0% -> 5%
where the time goes in v1:
time: 736 us; the launch traced here: 738 us
  waiting for transfers between devices  255 us (35%)
  starting transfers between devices  200 us (27%)
  other arithmetic  94.3 us (13%)
  matrix products  92.5 us (13%)
  local copies, waits for them, and re-layouts  47.3 us (6%)
  Pallas kernels  39.3 us (5%)
    ppermute x36, starting transfers between devices, line(): return lax.ppermute(x, 'fsdp', perm)  178 us
    ppermute x17, waiting for transfers between devices, swap(): return lax.ppermute(x, axis, [(0, 1), (1, 0)])  161 us
    ppermute x36, waiting for transfers between devices, line(): return lax.ppermute(x, 'fsdp', perm)  93.8 us
    dot_general x21, matrix products, dot(): return lax.dot_general(a, b, (dims, ((), ())), preferred_element_type=F32)  91.6 us
    select_n x3, other arithmetic, in_order(): jnp.where(index == 0, jnp.concatenate((mine, other), axis=axis), jnp.conc...  25.8 us
    pallas_call x1, Pallas kernels, attend_back(): pl.pallas_call(functools.partial(attend_back_kernel, row_tile(rows)), gri...  23.2 us
    unnamed x163, local copies, waits for them, and re-layouts  21 us
    ppermute x17, starting transfers between devices, swap(): return lax.ppermute(x, axis, [(0, 1), (1, 0)])  20.8 us
  transfers between devices with their start and end apart: 59, of which 27 were waited for; matrix products, arithmetic and copies ran while one was open for 17% of the time, Pallas kernels for 5%

profile of v1, /device:TPU:0, one launch (start us, length us, event | category | flops | bytes accessed | tf_op | source)
XLA Modules:
  0.0 737.8 jit_solution(1157677428040658968)
XLA Ops:
  29.4 8.0 %collective-permute-start.9 = (bf16[288,896]{1,0:T(8,128)(2,1)}, bf16[288,896]{1,0:T(8,128)(2,1)}, u32[]{:S(2)}, u32[]{:S(2)}) collective-permute-start(bf16[288,896]{1,0:T(8,128)(2,1)} %fusion.103), channel_id=1, source_target_pairs={{0,8},{4,12},{8,16},{12,20},{16,24},{20,28},{1,9},{5,13},{9,17},{1... | collective-permute-start | bytes 1548296 | tf_op jit(solution)/shard_map/ppermute | solution.py:86
  48.3 6.0 collective-permute-done.12
  66.2 12.4 %collective-permute-done.5 = bf16[96,1664]{1,0:T(8,128)(2,1)S(1)} collective-permute-done((bf16[96,1664]{1,0:T(8,128)(2,1)}, bf16[96,1664]{1,0:T(8,128)(2,1)S(1)}, u32[]{:S(2)}, u32[]{:S(2)}) %collective-permute-start.5) | collective-permute-done | bytes 319520 | tf_op jit(solution)/shard_map/ppermute | solution.py:86
  106.3 56.5 %collective-permute-done.7 = bf16[576,768]{1,0:T(8,128)(2,1)} collective-permute-done((bf16[576,768]{1,0:T(8,128)(2,1)}, bf16[576,768]{1,0:T(8,128)(2,1)}, u32[]{:S(2)}, u32[]{:S(2)}) %collective-permute-start.7) | collective-permute-done | bytes 884768 | tf_op jit(solution)/shard_map/ppermute | solution.py:46
  165.2 16.2 %attend.1 = (bf16[576,384]{1,0:T(8,128)(2,1)S(1)}, bf16[6,576,1152]{2,1,0:T(8,128)(2,1)}) custom-call(bf16[576,1152]{1,0:T(8,128)(2,1)S(1)} %convolution_convert_fusion.9.q_ref, bf16[1152,768]{1,0:T(8,128)(2,1)S(1)} %maximum_select_fusion.3.k_ref.v_ref, bf16[1152,768]{1,0:T(8,128)(2,1)S(1)} %maximum_select_fusion.3.k_ref.v_ref, ...), custom_call_target="tpu_custom_call" | custom-call | flops 2038431744 | bytes 7962624 | tf_op jit(solution)/shard_map/attend/pallas_call | solution.py:216
  187.1 8.4 %collective-permute-done.8 = bf16[288,768]{1,0:T(8,128)(2,1)S(1)} collective-permute-done((bf16[288,768]{1,0:T(8,128)(2,1)S(1)}, bf16[288,768]{1,0:T(8,128)(2,1)S(1)}, u32[]{:S(2)}, u32[]{:S(2)}) %collective-permute-start.8) | collective-permute-done | bytes 442400 | tf_op jit(solution)/shard_map/ppermute | solution.py:46
  210.1 20.3 %maximum_select_fusion = bf16[3072,768]{1,0:T(8,128)(2,1)S(1)} fusion(bf16[3072,384]{1,0:T(8,128)(2,1)} %collective-permute-done.17, bf16[1536,384]{1,0:T(8,128)(2,1)S(1)} %copy-done.17, bf16[1536,384]{1,0:T(8,128)(2,1)S(1)} %bitcast.304, pred[]{:T(512)S(6)} %eq.69), kind=kLoop, calls=%fused_computation.86 | loop fusion | flops 30670848 | bytes 9437185 | tf_op jit(solution)/shard_map/jit(_where)/select_n | solution.py:50
  234.9 9.3 %collective-permute-done.22 = bf16[288,768]{1,0:T(8,128)(2,1)S(1)} collective-permute-done((bf16[288,768]{1,0:T(8,128)(2,1)S(1)}, bf16[288,768]{1,0:T(8,128)(2,1)S(1)}, u32[]{:S(2)}, u32[]{:S(2)}) %collective-permute-start.22) | collective-permute-done | bytes 442400 | tf_op jit(solution)/shard_map/ppermute | solution.py:86
  245.9 9.2 %collective-permute-done.23 = bf16[288,768]{1,0:T(8,128)(2,1)S(1)} collective-permute-done((bf16[288,768]{1,0:T(8,128)(2,1)S(1)}, bf16[288,768]{1,0:T(8,128)(2,1)S(1)}, u32[]{:S(2)}, u32[]{:S(2)}) %collective-permute-start.23) | collective-permute-done | bytes 442400 | tf_op jit(solution)/shard_map/ppermute | solution.py:86
  269.1 86.9 %conditional.4 = (bf16[768,1536]{1,0:T(8,128)(2,1)}, f32[2304,768]{1,0:T(8,128)}, f32[768,1536]{1,0:T(8,128)}, bf16[1,1536,768]{2,1,0:T(8,128)(2,1)}, bf16[1,153...) conditional(s32[]{:T(128)} %convert_element_type.490, (bf16[2304,768]{1,0:T(8,128)(2,1)}, ...), branch_computations={%region_12.13_spmd, %region_13.14_spmd} | conditional | flops 65513521152 | bytes 383385792
  289.0 6.3 fusion.47
  316.8 8.2 %fusion.40 = (bf16[768,1536]{1,0:T(8,128)(2,1)}, f32[768,1536]{1,0:T(8,128)}) fusion(f32[768,1536]{1,0:T(8,128)S(1)} %fusion.158, bf16[768,768]{1,0:T(8,128)(2,1)S(1)} %fusion.59, bf16[768,1536]{1,0:T(8,128)(2,1)} %get-tuple-element.106), kind=kOutput, calls=%fused_computation.50 | convolution fusion | flops 1835532288 | bytes 15335424 | tf_op jit(solution)/shard_map/cond/branch_1_fun/dot_general | solution.py:21
  325.0 9.8 %fusion.20 = bf16[2304,768]{1,0:T(8,128)(2,1)} fusion(s32[2304]{0:T(1024)S(1)} %add_bitcast_fusion, pred[2304]{0:T(1024)(128)(4,1)S(1)} %get-tuple-element.102, f32[768,768]{1,0:T(8,128)} %fusion.160, bf16[768,1536]{1,0:T(8,128)(2,1)} %get-tuple-element.297, bf16[768,1536]{1,0:T(8,128)(2,1)} %get-tuple-element.106), kind=kOutput, calls=%fused_computation.34 | convolution fusion | flops 4534566912 | bytes 10628352 | tf_op jit(solution)/shard_map/cond/branch_1_fun/dot_general | solution.py:21
  344.2 11.7 %fusion.31 = f32[2304,768]{1,0:T(8,128)} fusion(s32[2304]{0:T(1024)S(1)} %add_bitcast_fusion, pred[2304]{0:T(1024)(128)(4,1)S(1)} %get-tuple-element.102, f32[768,768]{1,0:T(8,128)} %fusion.65, bf16[1536,768]{1,0:T(8,128)(2,1)} %get-tuple-element.105, f32[768,1536]{1,0:T(8,128)} %get-tuple-element.298), kind=kOutput, calls=%fused_computation.43 | convolution fusion | flops 4548722688 | bytes 16526592 | tf_op jit(solution)/shard_map/cond/branch_1_fun/dot_general | solution.py:21
  369.0 92.1 %collective-permute-start.36 = (bf16[288,768]{1,0:T(8,128)(2,1)}, bf16[288,768]{1,0:T(8,128)(2,1)}, u32[]{:S(2)}, u32[]{:S(2)}) collective-permute-start(bf16[288,768]{1,0:T(8,128)(2,1)} %get-tuple-element.310), channel_id=1, source_target_pairs={{0,8},{4,12},{1,9},{5,13},{2,10},{6,14},{3,11},{7,15}} | collective-permute-start | bytes 1327112 | tf_op jit(solution)/shard_map/ppermute | solution.py:86
  492.1 6.5 collective-permute-done.29
  517.1 9.3 %collective-permute-done.41 = bf16[288,768]{1,0:T(8,128)(2,1)S(1)} collective-permute-done((bf16[288,768]{1,0:T(8,128)(2,1)S(1)}, bf16[288,768]{1,0:T(8,128)(2,1)S(1)}, u32[]{:S(2)}, u32[]{:S(2)}) %collective-permute-start.41) | collective-permute-done | bytes 442400 | tf_op jit(solution)/shard_map/ppermute | solution.py:86
  526.9 6.3 collective-permute-done.33
  544.9 23.2 %attend_back.1 = (bf16[576,384]{1,0:T(8,128)(2,1)S(1)}, bf16[1152,384]{1,0:T(8,128)(2,1)S(1)}, bf16[1152,384]{1,0:T(8,128)(2,1)S(1)}, f32[3,2,8,1152]{3,2,1,0:T(8,128)S(1)}) custom-call(bf16[576,1152]{1,0:T(8,128)(2,1)S(1)} %convolution_convert_fusion.9.q_ref, bf16[1152,768]{1,0:T(8,128)(2,1)S(1)} %copy-done.1, bf16[1152,768]{1,0:T(8,128)(2,1)S(1)} %copy-done.1, ...), custom_call_target="tpu_custom_call" | custom-call | flops 4076863488 | bytes 7962624 | tf_op jit(solution)/shard_map/attend_back/pallas_call | solution.py:249
  570.8 36.8 %collective-permute-done.43 = bf16[576,768]{1,0:T(8,128)(2,1)S(1)} collective-permute-done((bf16[576,768]{1,0:T(8,128)(2,1)S(1)}, bf16[576,768]{1,0:T(8,128)(2,1)S(1)}, u32[]{:S(2)}, u32[]{:S(2)}) %collective-permute-start.43) | collective-permute-done | bytes 884768 | tf_op jit(solution)/shard_map/ppermute | solution.py:46
  634.0 6.3 collective-permute-start.48
  651.9 30.0 %collective-permute-done.55 = bf16[768,1536]{1,0:T(8,128)(2,1)S(1)} collective-permute-done((bf16[768,1536]{1,0:T(8,128)(2,1)}, bf16[768,1536]{1,0:T(8,128)(2,1)S(1)}, u32[]{:S(2)}, u32[]{:S(2)}) %collective-permute-start.55) | collective-permute-done | bytes 2359328 | tf_op jit(solution)/shard_map/ppermute | solution.py:46
  685.3 21.5 %collective-permute-done.58 = bf16[1536,384]{1,0:T(8,128)(2,1)S(1)} collective-permute-done((bf16[1536,384]{1,0:T(8,128)(2,1)S(1)}, bf16[1536,384]{1,0:T(8,128)(2,1)S(1)}, u32[]{:S(2)}, u32[]{:S(2)}) %collective-permute-start.58) | collective-permute-done | bytes 1179680 | tf_op jit(solution)/shard_map/ppermute | solution.py:46
  709.8 6.3 collective-permute-start.50
  (424 shorter events, 307.7 us)
Async XLA Ops:
  19.0 21.5 %collective-permute-start.3 = (bf16[96,1664]{1,0:T(8,128)(2,1)}, bf16[96,1664]{1,0:T(8,128)(2,1)}, u32[]{:S(2)}, u32[]{:S(2)}) collective-permute-start(bf16[96,1664]{1,0:T(8,128)(2,1)} %pad_maximum_fusion.6), channel_id=1, source_target_pairs={{8,0},{12,4},{16,8},{20,12},{24,16},{28,20},{9,1},{13,5},{17,9},{2... | collective-permute-start | bytes 958472 | tf_op jit(solution)/shard_map/ppermute | solution.py:86
  38.7 52.2 %collective-permute-start.25 = (bf16[384,1536]{1,0:T(8,128)(2,1)}, bf16[384,1536]{1,0:T(8,128)(2,1)}, u32[]{:S(2)}, u32[]{:S(2)}) collective-permute-start(bf16[384,1536]{1,0:T(8,128)(2,1)} %bitcast.315), channel_id=1, source_target_pairs={{0,2},{2,0},{1,3},{3,1},{4,6},{6,4},{5,7},{7,5},{8,10},{10,8},{9,1... | collective-permute-start | bytes 3538952 | tf_op jit(solution)/shard_map/ppermute | solution.py:46
  46.8 40.8 %collective-permute-start.16 = (bf16[1536,384]{1,0:T(8,128)(2,1)S(1)}, bf16[1536,384]{1,0:T(8,128)(2,1)S(1)}, u32[]{:S(2)}, u32[]{:S(2)}) collective-permute-start(bf16[1536,384]{1,0:T(8,128)(2,1)S(1)} %bitcast.302), channel_id=1, source_target_pairs={{0,1},{1,0},{2,3},{3,2},{4,5},{5,4},{6,7},{7,6},{8,9},{9,8},{10,11... | collective-permute-start | bytes 3538952 | tf_op jit(solution)/shard_map/ppermute | solution.py:46
  54.3 31.1 %collective-permute-start.10 = (bf16[288,896]{1,0:T(8,128)(2,1)}, bf16[288,896]{1,0:T(8,128)(2,1)}, u32[]{:S(2)}, u32[]{:S(2)}) collective-permute-start(bf16[288,896]{1,0:T(8,128)(2,1)} %collective-permute-done.9), channel_id=1, source_target_pairs={{8,16},{12,20},{16,24},{20,28},{9,17},{13,21},{17,25},{21,29},{10,... | collective-permute-start | bytes 1548296 | tf_op jit(solution)/shard_map/ppermute | solution.py:86
  58.6 27.6 %collective-permute-start.13 = (bf16[288,896]{1,0:T(8,128)(2,1)}, bf16[288,896]{1,0:T(8,128)(2,1)}, u32[]{:S(2)}, u32[]{:S(2)}) collective-permute-start(bf16[288,896]{1,0:T(8,128)(2,1)} %collective-permute-done.12), channel_id=1, source_target_pairs={{8,0},{12,4},{16,8},{20,12},{9,1},{13,5},{17,9},{21,13},{10,2},{14... | collective-permute-start | bytes 1548296 | tf_op jit(solution)/shard_map/ppermute | solution.py:86
  86.2 116.1 %collective-permute-start.14 = (bf16[288,896]{1,0:T(8,128)(2,1)}, bf16[288,896]{1,0:T(8,128)(2,1)}, u32[]{:S(2)}, u32[]{:S(2)}) collective-permute-start(bf16[288,896]{1,0:T(8,128)(2,1)} %collective-permute-done.13), channel_id=1, source_target_pairs={{8,0},{12,4},{9,1},{13,5},{10,2},{14,6},{11,3},{15,7}} | collective-permute-start | bytes 1548296 | tf_op jit(solution)/shard_map/ppermute | solution.py:86
  89.4 120.6 %collective-permute-start.17 = (bf16[3072,384]{1,0:T(8,128)(2,1)}, bf16[3072,384]{1,0:T(8,128)(2,1)}, u32[]{:S(2)}, u32[]{:S(2)}) collective-permute-start(bf16[3072,384]{1,0:T(8,128)(2,1)} %pad_maximum_fusion.2), channel_id=1, source_target_pairs={{0,2},{2,0},{1,3},{3,1},{4,6},{6,4},{5,7},{7,5},{8,10},{10,8},{9,1... | collective-permute-start | bytes 7077896 | tf_op jit(solution)/shard_map/ppermute | solution.py:46
  94.0 175.2 %collective-permute-start.26 = (bf16[768,1536]{1,0:T(8,128)(2,1)}, bf16[768,1536]{1,0:T(8,128)(2,1)}, u32[]{:S(2)}, u32[]{:S(2)}) collective-permute-start(bf16[768,1536]{1,0:T(8,128)(2,1)} %maximum_select_fusion.2), channel_id=1, source_target_pairs={{0,1},{1,0},{2,3},{3,2},{4,5},{5,4},{6,7},{7,6},{8,9},{9,8},{10,11... | collective-permute-start | bytes 7077896 | tf_op jit(solution)/shard_map/ppermute | solution.py:46
  101.4 61.4 %collective-permute-start.7 = (bf16[576,768]{1,0:T(8,128)(2,1)}, bf16[576,768]{1,0:T(8,128)(2,1)}, u32[]{:S(2)}, u32[]{:S(2)}) collective-permute-start(bf16[576,768]{1,0:T(8,128)(2,1)} %slice.281), channel_id=1, source_target_pairs={{0,2},{2,0},{1,3},{3,1},{4,6},{6,4},{5,7},{7,5},{8,10},{10,8},{9,1... | collective-permute-start | bytes 2654216 | tf_op jit(solution)/shard_map/ppermute | solution.py:46
  203.5 51.8 %collective-permute-start.15 = (bf16[4,288,896]{2,1,0:T(8,128)(2,1)S(1)}, bf16[4,288,896]{2,1,0:T(8,128)(2,1)S(1)}, u32[]{:S(2)}, u32[]{:S(2)}) collective-permute-start(bf16[4,288,896]{2,1,0:T(8,128)(2,1)S(1)} %constant_dynamic-slice_fusion.4), channel_id=1, source_target_pairs={{0,4},{4,0},{8,12},{12,8},{16,20},{20,16},{24,28},{28,24},{1,5},{5... | collective-permute-start | bytes 6193160 | tf_op jit(solution)/shard_map/ppermute | solution.py:81
  203.6 26.8 %collective-permute-start.21 = (bf16[288,768]{1,0:T(8,128)(2,1)S(1)}, bf16[288,768]{1,0:T(8,128)(2,1)S(1)}, u32[]{:S(2)}, u32[]{:S(2)}) collective-permute-start(bf16[288,768]{1,0:T(8,128)(2,1)S(1)} %multiply_convert_fusion.16), channel_id=1, source_target_pairs={{8,0},{12,4},{16,8},{20,12},{24,16},{28,20},{9,1},{13,5},{17,9},{2... | collective-permute-start | bytes 1327112 | tf_op jit(solution)/shard_map/ppermute | solution.py:86
  209.2 22.6 %collective-permute-start.19 = (bf16[288,768]{1,0:T(8,128)(2,1)S(1)}, bf16[288,768]{1,0:T(8,128)(2,1)S(1)}, u32[]{:S(2)}, u32[]{:S(2)}) collective-permute-start(bf16[288,768]{1,0:T(8,128)(2,1)S(1)} %collective-permute-done.18), channel_id=1, source_target_pairs={{8,16},{12,20},{16,24},{20,28},{9,17},{13,21},{17,25},{21,29},{10,... | collective-permute-start | bytes 1327112 | tf_op jit(solution)/shard_map/ppermute | solution.py:86
  364.9 96.1 %collective-permute-start.27 = (bf16[4,288,768]{2,1,0:T(8,128)(2,1)}, bf16[4,288,768]{2,1,0:T(8,128)(2,1)}, u32[]{:S(2)}, u32[]{:S(2)}) collective-permute-start(bf16[4,288,768]{2,1,0:T(8,128)(2,1)} %bitcast.48), channel_id=1, source_target_pairs={{0,4},{4,0},{8,12},{12,8},{16,20},{20,16},{24,28},{28,24},{1,5},{5... | collective-permute-start | bytes 5308424 | tf_op jit(solution)/shard_map/ppermute | solution.py:81
  369.0 102.2 %collective-permute-start.36 = (bf16[288,768]{1,0:T(8,128)(2,1)}, bf16[288,768]{1,0:T(8,128)(2,1)}, u32[]{:S(2)}, u32[]{:S(2)}) collective-permute-start(bf16[288,768]{1,0:T(8,128)(2,1)} %get-tuple-element.310), channel_id=1, source_target_pairs={{0,8},{4,12},{1,9},{5,13},{2,10},{6,14},{3,11},{7,15}} | collective-permute-start | bytes 1327112 | tf_op jit(solution)/shard_map/ppermute | solution.py:86
  467.1 20.7 %collective-permute-start.39 = (bf16[288,768]{1,0:T(8,128)(2,1)}, bf16[288,768]{1,0:T(8,128)(2,1)}, u32[]{:S(2)}, u32[]{:S(2)}) collective-permute-start(bf16[288,768]{1,0:T(8,128)(2,1)} %get-tuple-element.311), channel_id=1, source_target_pairs={{24,16},{28,20},{25,17},{29,21},{26,18},{30,22},{27,19},{31,23}} | collective-permute-start | bytes 1327112 | tf_op jit(solution)/shard_map/ppermute | solution.py:86
  538.2 90.9 %collective-permute-start.57 = (bf16[2,1536,384]{2,1,0:T(8,128)(2,1)}, bf16[2,1536,384]{2,1,0:T(8,128)(2,1)}, u32[]{:S(2)}, u32[]{:S(2)}) collective-permute-start(bf16[2,1536,384]{2,1,0:T(8,128)(2,1)} %constant_dynamic-slice_fusion), channel_id=1, source_target_pairs={{0,2},{2,0},{1,3},{3,1},{4,6},{6,4},{5,7},{7,5},{8,10},{10,8},{9,1... | collective-permute-start | bytes 7077896 | tf_op jit(solution)/shard_map/ppermute | solution.py:46
  569.2 38.4 %collective-permute-start.43 = (bf16[576,768]{1,0:T(8,128)(2,1)S(1)}, bf16[576,768]{1,0:T(8,128)(2,1)S(1)}, u32[]{:S(2)}, u32[]{:S(2)}) collective-permute-start(bf16[576,768]{1,0:T(8,128)(2,1)S(1)} %constant_dynamic-slice_fusion.2), channel_id=1, source_target_pairs={{0,2},{2,0},{1,3},{3,1},{4,6},{6,4},{5,7},{7,5},{8,10},{10,8},{9,1... | collective-permute-start | bytes 2654216 | tf_op jit(solution)/shard_map/ppermute | solution.py:46
  627.6 54.3 %collective-permute-start.55 = (bf16[768,1536]{1,0:T(8,128)(2,1)}, bf16[768,1536]{1,0:T(8,128)(2,1)S(1)}, u32[]{:S(2)}, u32[]{:S(2)}) collective-permute-start(bf16[768,1536]{1,0:T(8,128)(2,1)} %get-tuple-element.139), channel_id=1, source_target_pairs={{0,1},{1,0},{2,3},{3,2},{4,5},{5,4},{6,7},{7,6},{8,9},{9,8},{10,11... | collective-permute-start | bytes 7077896 | tf_op jit(solution)/shard_map/ppermute | solution.py:46
  640.4 66.4 %collective-permute-start.58 = (bf16[1536,384]{1,0:T(8,128)(2,1)S(1)}, bf16[1536,384]{1,0:T(8,128)(2,1)S(1)}, u32[]{:S(2)}, u32[]{:S(2)}) collective-permute-start(bf16[1536,384]{1,0:T(8,128)(2,1)S(1)} %fusion.79), channel_id=1, source_target_pairs={{0,1},{1,0},{2,3},{3,2},{4,5},{5,4},{6,7},{7,6},{8,9},{9,8},{10,11... | collective-permute-start | bytes 3538952 | tf_op jit(solution)/shard_map/ppermute | solution.py:46
  641.1 43.1 %collective-permute-start.51 = (bf16[96,1664]{1,0:T(8,128)(2,1)S(1)}, bf16[96,1664]{1,0:T(8,128)(2,1)S(1)}, u32[]{:S(2)}, u32[]{:S(2)}) collective-permute-start(bf16[96,1664]{1,0:T(8,128)(2,1)S(1)} %get-tuple-element.319), channel_id=1, source_target_pairs={{24,16},{28,20},{25,17},{29,21},{26,18},{30,22},{27,19},{31,23}} | collective-permute-start | bytes 958472 | tf_op jit(solution)/shard_map/ppermute | solution.py:86
  647.5 36.7 %collective-permute-start.49 = (bf16[96,1664]{1,0:T(8,128)(2,1)S(1)}, bf16[96,1664]{1,0:T(8,128)(2,1)S(1)}, u32[]{:S(2)}, u32[]{:S(2)}) collective-permute-start(bf16[96,1664]{1,0:T(8,128)(2,1)S(1)} %fusion.97), channel_id=1, source_target_pairs={{0,8},{4,12},{8,16},{12,20},{1,9},{5,13},{9,17},{13,21},{2,10},{6,... | collective-permute-start | bytes 958472 | tf_op jit(solution)/shard_map/ppermute | solution.py:86
  682.8 45.6 %collective-permute-start.56 = (bf16[384,1536]{1,0:T(8,128)(2,1)S(1)}, bf16[384,1536]{1,0:T(8,128)(2,1)S(1)}, u32[]{:S(2)}, u32[]{:S(2)}) collective-permute-start(bf16[384,1536]{1,0:T(8,128)(2,1)S(1)} %dynamic-slice_convert_fusion), channel_id=1, source_target_pairs={{0,2},{2,0},{1,3},{3,1},{4,6},{6,4},{5,7},{7,5},{8,10},{10,8},{9,1... | collective-permute-start | bytes 3538952 | tf_op jit(solution)/shard_map/ppermute | solution.py:46
  684.5 31.6 %collective-permute-start.52 = (bf16[96,1664]{1,0:T(8,128)(2,1)S(1)}, bf16[96,1664]{1,0:T(8,128)(2,1)S(1)}, u32[]{:S(2)}, u32[]{:S(2)}) collective-permute-start(bf16[96,1664]{1,0:T(8,128)(2,1)S(1)} %get-tuple-element.317), channel_id=1, source_target_pairs={{16,8},{20,12},{24,16},{28,20},{17,9},{21,13},{25,17},{29,21},{18,... | collective-permute-start | bytes 958472 | tf_op jit(solution)/shard_map/ppermute | solution.py:86
  708.4 21.6 %collective-permute-start.34 = (bf16[288,768]{1,0:T(8,128)(2,1)S(1)}, bf16[288,768]{1,0:T(8,128)(2,1)S(1)}, u32[]{:S(2)}, u32[]{:S(2)}) collective-permute-start(bf16[288,768]{1,0:T(8,128)(2,1)S(1)} %copy-done.35), channel_id=1, source_target_pairs={{0,1},{1,0},{2,3},{3,2},{4,5},{5,4},{6,7},{7,6},{8,9},{9,8},{10,11... | collective-permute-start | bytes 1327112 | tf_op jit(solution)/shard_map/ppermute | solution.py:46
  (103 other events, 1834.1 us)
